TPU v7x, 256 devices: a whole 4x4x8 slice. The times are simulated.
256 devices in a mesh: freq: 2 (over core), xs: 64 (over z, y, x_hi), yh: 2 (over x_lo).
Axes of the slice: x: 4 (x_hi: 2, x_lo: 2; x = x_hi * 2 + x_lo), y: 4, z: 8, core: 2. Of those that a mesh axis runs over, the one named last changes fastest.
Arguments:
- field: float32 [2, 64, 1024, 2048], P(None, 'freq', 'xs', 'yh'), may hold values from -6 to 6
- spectral_phase: float32 [64, 2048], P('freq'), may hold values from -3.140625 to 3.140625
- chirp_shift: int32 [64], P('freq'), may hold values from -4 to 4, as said below
- tile_map: int32 [256], P('xs'), may hold values from 0 to 3
- tile_phase: float32 [4, 64], P(None, 'freq'), may hold values from -3.140625 to 3.140625
Outputs:
- pulse: float32 [2, 32, 1024, 2048], P(None, None, 'xs', ('freq', 'yh'))
Inputs may be any that keep to these rules, and one draw needn't show every extreme that they name: `chirp_shift`: some frequency has the offset 4 and another the offset -4.
All inputs are finite; a program needn't handle non-finite values.
Results may differ from a plain program's by a relative error of at most 0.0003.
Values sent between devices are 32-bit elements; how exact they have to be, the bound alone decides.
A program may use at most 128 MiB of HBM per device.

v0:
```python
import functools
import math

import jax
import jax.numpy as jnp
import numpy as np
from jax import lax
from jax.experimental import pallas as pl
from jax.experimental.pallas import tpu as pltpu
from jax.sharding import PartitionSpec as P

NF = 64
NY = 2048
NT = 32
VMEM = 60
BF = jnp.bfloat16
F32 = jnp.float32
AXES = ("freq", "xs", "yh")
MESH = pl.DeviceIdType.MESH


def dft_tables():
    m = np.arange(256)
    angle = 2.0 * np.pi * (np.outer(m, m) % 256) / 256
    waves = np.stack([np.cos(angle), np.sin(angle)]) / math.sqrt(NY)
    odd_order = np.concatenate([np.arange(64) + 64 * b for b in (1, 0, 3, 2)])
    turn = 2.0 * np.pi * np.outer(np.arange(8), m) / NY
    twiddle = np.stack([np.cos(turn), np.sin(turn)])
    return np.stack([waves, waves[:, :, odd_order]]).astype(np.float32), twiddle.astype(np.float32)


def split(value):
    high = value.astype(BF)
    return high, (value - high.astype(F32)).astype(BF)


def dot(a, b):
    return jnp.dot(a, b, preferred_element_type=F32)


def dot_t(a, b):
    return lax.dot_general(a, b, (((1,), (1,)), ((), ())), preferred_element_type=F32)


def sincos(x):
    k = jnp.floor(x * (2.0 / math.pi) + 0.5)
    r = ((x - k * 1.5703125) - k * 4.837512969970703125e-4) - k * 7.54978995489188216e-8
    z = r * r
    sine = r + r * z * (-1.6666654611e-1 + z * (8.3321608736e-3 - z * 1.9515295891e-4))
    cosine = (1.0 - 0.5 * z) + z * z * (4.166664568298827e-2 + z * (-1.388731625493765e-3 + z * 2.443315711809948e-5))
    half = jnp.floor(k * 0.5)
    swap = (k - 2.0 * half) > 0.5
    sign = 1.0 - 2.0 * (half - 2.0 * jnp.floor(half * 0.5))
    return sign * jnp.where(swap, cosine, sine), sign * jnp.where(swap, -sine, cosine)


def butterflies(re, im, tw):
    a = [(re[:, 256 * c : 256 * c + 256], im[:, 256 * c : 256 * c + 256]) for c in range(4)]
    r = math.sqrt(0.5)

    def add(u, v):
        return u[0] + v[0], u[1] + v[1]

    def sub(u, v):
        return u[0] - v[0], u[1] - v[1]

    def mi(u):
        return u[1], -u[0]

    def four(b):
        e0, e1 = add(b[0], b[2]), sub(b[0], b[2])
        e2, e3 = add(b[1], b[3]), mi(sub(b[1], b[3]))
        return add(e0, e2), add(e1, e3), sub(e0, e2), sub(e1, e3)

    even = four(a)
    b1 = ((a[1][0] + a[1][1]) * r, (a[1][1] - a[1][0]) * r)
    b3 = ((a[3][1] - a[3][0]) * r, (-a[3][0] - a[3][1]) * r)
    odd = four((a[0], b1, mi(a[2]), b3))
    both = []
    for side, parts in enumerate((even, odd)):
        row = []
        for j in range(4):
            p = 2 * j + side
            u = parts[j]
            if p:
                c, s = tw[0, p : p + 1, :], tw[1, p : p + 1, :]
                u = u[0] * c + u[1] * s, u[1] * c - u[0] * s
            row.append(u)
        both.append(row)
    return both


def kernel(
    strips, field, phi_hbm, waves_hbm, tw_hbm, shift_row, tile_phase, tile_ids, out,
    flat, snd, keep, other, halo_a, halo_b, prm, prm_out, prm_in, prm_pair,
    phi, waves, tw, e_own, e_other, table, perm, ww, wh,
    spread, spec, near, near_in, side, side_in, pp, opp, relay_in, cross, cross_in, via_1, via_2, *rest,
):
    (load_sem, snd_s, snd_r, ha_s, ha_r, hb_s, hb_r, prm_s, prm_r,
     near_s, near_r, row_s, row_r, rel_s, rel_r, crs_s, crs_r, v1_s, v1_r, v2_s, v2_r) = rest
    g, s, h = (lax.axis_index(a) for a in AXES)
    odd = lax.rem(s, 2)
    pair = s + 1 - 2 * odd
    onward = lax.rem(s + strips + 4 * odd - 2, strips)
    back = lax.rem(s + strips + 2 - 4 * odd, strips)
    core = (1 - g, s, h)

    z, y, turns = s // 8, lax.rem(s // 2, 4), strips // 8
    hop = 1 - 2 * odd
    across = 8 * z + 2 * lax.rem(y + 4 + hop, 4) + odd
    across_from = 8 * z + 2 * lax.rem(y + 4 - hop, 4) + odd
    z_on = 8 * lax.rem(z + turns - hop, turns) + odd
    z_back = 8 * lax.rem(z + turns + hop, turns) + odd
    leaves = (y == 2 - odd).astype(jnp.int32)
    third = across + leaves * (z_on + 2 * (3 - 3 * odd) - across)
    enters = (y == 3 - 3 * odd).astype(jnp.int32)
    third_from = across_from + enters * (z_back + 2 * (2 - odd) - across_from)

    def peer(dg, ds, dh):
        return (lax.rem(g + dg, 2), pair if ds else s, lax.rem(h + dh, 2))

    def remote(src, dst, a, b, to):
        return pltpu.make_async_remote_copy(
            src_ref=src, dst_ref=dst, send_sem=a, recv_sem=b, device_id=to, device_id_type=MESH
        )

    def block_of(n):
        return n + odd * (3 - 2 * n)

    loads = [
        pltpu.make_async_copy(field.at[:, :, pl.ds(128 * y, 128)], flat.at[y], load_sem.at[y]) for y in range(8)
    ]
    tables = [
        pltpu.make_async_copy(src, dst, load_sem.at[8 + k])
        for k, (src, dst) in enumerate(((waves_hbm, waves), (tw_hbm, tw), (phi_hbm, phi)))
    ]
    for c in loads + tables:
        c.start()
    barrier = pltpu.get_barrier_semaphore()
    greet = [core, peer(0, 0, 1), peer(1, 0, 1), peer(0, 1, 1), peer(1, 1, 1), (g, onward, h), (g, back, h)]
    greet += [(g, across, h), (g, across_from, h), (g, third, h), (g, third_from, h)]
    for to in greet:
        pl.semaphore_signal(barrier, inc=1, device_id=to, device_id_type=MESH)

    def snd_copy(i):
        return remote(snd.at[i], other.at[i], snd_s.at[i], snd_r.at[i], core)

    def a_copy(i):
        return remote(keep.at[i], halo_a.at[i], ha_s.at[i], ha_r.at[i], (g, onward, h))

    def b_copy(i):
        return remote(other.at[i], halo_b.at[i], hb_s.at[i], hb_r.at[i], (g, onward, h))

    def via_copy(hops, k, which):
        i = 4 + 3 * k
        if hops == 1:
            src = (keep, other)[which].at[i]
            return remote(src, via_1.at[k, which], v1_s.at[k, which], v1_r.at[k, which], (g, across, h))
        if hops == 2:
            return remote(
                via_1.at[k, which], via_2.at[k, which], v2_s.at[k, which], v2_r.at[k, which], (g, across, h)
            )
        dst, sems = ((halo_a, (ha_s, ha_r)), (halo_b, (hb_s, hb_r)))[which]
        return remote(via_2.at[k, which], dst.at[i], sems[0].at[i], sems[1].at[i], (g, third, h))

    def pass_on(hops, k):
        for which in range(2):
            via_copy(hops - 1, k, which).wait_recv()
            via_copy(hops, k, which).start()

    def gather_rows(i, whose, into):
        row = 4 * block_of(lax.rem(i, 4)) + 2 * whose + i // 4
        for c in range(2):
            for y in range(8):
                into[i, c, :, 128 * y : 128 * y + 128] = flat[y, c, pl.ds(row, 32, stride=16), :]

    gap = jnp.zeros((8, 32), F32)
    rows = jnp.concatenate([shift_row[...].astype(F32), tile_phase[...], jnp.zeros((3, 32), F32)], axis=0)
    prm[0:8, :] = jnp.concatenate([rows, gap, rows, gap], axis=1)
    for rb in range(4):
        prm[8 + rb : 9 + rb, :] = jnp.full((1, 128), tile_ids[rb], jnp.int32).astype(F32)
    prm[12:16, :] = jnp.zeros((4, 128), F32)
    prm_out[...] = pltpu.roll(prm[...], 32, 1)
    prm_core = remote(prm_out, prm_in, prm_s.at[0], prm_r.at[0], core)
    prm_strip = remote(prm, prm_pair, prm_s.at[1], prm_r.at[1], peer(0, 1, 1))

    for c in loads:
        c.wait()

    def pack_send(i, carry):
        gather_rows(i, 1 - g, snd)
        snd_copy(i).start()
        return carry

    def pack_keep(i, carry):
        gather_rows(i, g, keep)
        return carry

    for i in (0, 4, 1):
        gather_rows(i, g, keep)
    pl.semaphore_wait(barrier, len(greet))
    a_copy(0).start()
    via_copy(1, 0, 0).start()
    a_copy(1).start()
    lax.fori_loop(0, 8, pack_send, 0)
    prm_core.start()
    prm_strip.start()
    lax.fori_loop(2, 4, pack_keep, 0)
    lax.fori_loop(5, 8, pack_keep, 0)
    for i in (0, 4, 1):
        snd_copy(i).wait_recv()
        if i == 4:
            via_copy(1, 0, 1).start()
        else:
            b_copy(i).start()

    for c in tables:
        c.wait()
    lane = lax.broadcasted_iota(jnp.int32, (512, 1), 0)
    wave = lax.broadcasted_iota(jnp.int32, (1, 512), 1)
    turn = lax.rem(lane, 128)
    for half in range(2):
        late = (turn >= 64).astype(jnp.int32)
        late = late if half == 0 else 1 - late
        target = 8 * lax.rem(turn, 64) + 2 * (lane // 128) + late
        perm[half] = jnp.where(target == wave, 1.0, 0.0).astype(BF)
        c_hi, c_lo = split(waves[half, 0])
        s_hi, s_lo = split(waves[half, 1])
        for k, (c, w) in enumerate(((c_hi, s_hi), (c_hi, s_hi), (c_lo, s_lo))):
            table[half, 512 * k : 512 * k + 256, 0:256] = c
            table[half, 512 * k : 512 * k + 256, 256:512] = -w
            table[half, 512 * k + 256 : 512 * k + 512, 0:256] = w
            table[half, 512 * k + 256 : 512 * k + 512, 256:512] = c

    lanes = lax.rem(lax.broadcasted_iota(jnp.int32, (1, 512), 1), 128)
    for half in range(2):
        late = lanes >= 64 if half == 0 else lanes < 64
        sign = 1.0 - 2.0 * jnp.where(late, h, 0).astype(F32)
        stack = []
        for b in (half, half + 2):
            sine, cosine = sincos(phi[:, 512 * b : 512 * b + 512])
            stack += [*split(cosine), *split(sine)]
        got = dot_t(jnp.concatenate(stack, axis=0), perm[half])
        for k, b in enumerate((half, half + 2)):
            for part in range(2):
                at = 128 * k + 64 * part
                e_own[part, :, 512 * b : 512 * b + 512] = (got[at : at + 32] + got[at + 32 : at + 64]) * sign
    e_copy = remote(e_own, e_other, prm_s.at[2], prm_r.at[2], core)
    e_copy.start()

    prm_core.wait()
    prm_strip.wait()
    both = prm[...] + prm_in[...]
    shift = both[0:1, :]
    col = lax.broadcasted_iota(jnp.int32, (NT, 128), 1)
    freq = lax.rem(lax.rem(col, 64) + 32 * g, NF)
    angle = (2.0 * math.pi / NF) * lax.rem(lax.broadcasted_iota(jnp.int32, (NT, 128), 0) * freq, NF).astype(F32)
    scale = 1.0 / math.sqrt(NF)
    real_in = col < 64

    def base(tile):
        phase = jnp.zeros((1, 128), F32)
        for t in range(4):
            phase = phase + jnp.where(tile == float(t), both[1 + t : 2 + t, :], 0.0)
        im, re = sincos(angle + phase)
        im, re = im * scale, re * scale
        return jnp.concatenate([jnp.where(real_in, re, -im), jnp.where(real_in, im, re)], axis=0)

    far = (4 * (1 - 2 * odd)).astype(F32)
    inside = jnp.where(odd == 1, (s > 1).astype(F32), (s < strips - 2).astype(F32))
    for nd in range(4):
        dest = block_of(nd)
        here, there = base(prm[8 + nd : 9 + nd, :]), base(prm_pair[pl.ds(8 + dest, 1), :])
        rows = slice(64 * nd, 64 * nd + 64)
        for n in range(4):
            source = block_of(n)
            own_hi, own_lo = split(jnp.where(shift == (nd - source).astype(F32), here, 0.0))
            step = (dest - source).astype(F32)
            pair_hi, pair_lo = split(jnp.where(shift == step + far, there, 0.0))
            halo_hi, halo_lo = split(jnp.where(shift == step - far, there * inside, 0.0))
            below = slice(256 + 64 * nd, 320 + 64 * nd)
            for k, (u, v, w) in enumerate(
                ((own_hi, pair_hi, halo_hi), (own_hi, pair_hi, halo_hi), (own_lo, pair_lo, halo_lo))
            ):
                at = 512 * k + 128 * n
                ww[rows, at : at + 128] = u
                ww[below, at : at + 128] = v
                wh[n, rows, 128 * k : 128 * k + 128] = w
    for i in (2, 3, 5, 6, 7):
        snd_copy(i).wait_recv()
    e_copy.wait()

    def spectrum(a, b, i, at, depth):
        re = jnp.concatenate([a[i, 0], b[i, 0]], axis=0)
        im = jnp.concatenate([a[i, 1], b[i, 1]], axis=0)
        for half_p, parts in enumerate(butterflies(re, im, tw)):
            for j, pieces in enumerate(parts):
                for half, w in enumerate(pieces):
                    hi, lo = split(w)
                    for k, x in enumerate((hi, lo, hi)):
                        at_k = 512 * k + 256 * half
                        spread[half_p, 64 * j : 64 * j + 64, at_k : at_k + 256] = x
        even, uneven = (dot(spread[k], table[k]) for k in range(2))
        early = lax.broadcasted_iota(jnp.int32, (64, 128), 1) < 64
        for j in range(4):
            for b4 in range(4):
                first, second = (even, uneven) if b4 % 2 == 0 else (uneven, even)
                rows = slice(64 * j, 64 * j + 64)
                c0 = 128 * (b4 // 2)
                u = jnp.where(early, first[rows, c0 : c0 + 128], second[rows, c0 : c0 + 128])
                v = jnp.where(early, first[rows, 256 + c0 : 384 + c0], second[rows, 256 + c0 : 384 + c0])
                e0 = 512 * b4 + 128 * j
                c, w = (
                    jnp.concatenate([e_own[part, :, e0 : e0 + 128], e_other[part, :, e0 : e0 + 128]], axis=0)
                    for part in range(2)
                )
                for half, value in enumerate((u * c - v * w, u * w + v * c)):
                    hi, lo = split(value)
                    for k, x in enumerate((hi, lo, hi)):
                        spec[b4, pl.ds(k * depth + at + 64 * half, 64), 128 * j : 128 * j + 128] = x

    def block_at(dg, dh):
        return 2 * lax.rem(g + dg, 2) + lax.rem(h + dh, 2)

    def near_copy(ii):
        return remote(near.at[1, ii], near_in.at[ii], near_s.at[ii], near_r.at[ii], core)

    def dest_rows(n):
        return pl.ds(pl.multiple_of(64 * (3 - block_of(n)), 64), 64)

    def row_copy(dg, i):
        at, ii = dest_rows(lax.rem(i, 4)), i // 4
        return remote(side.at[dg, ii, at], side_in.at[dg, ii, at], row_s.at[dg, i], row_r.at[dg, i], peer(dg, 0, 1))

    def opp_cross(i):
        return remote(opp.at[i], relay_in.at[i], rel_s.at[i], rel_r.at[i], peer(0, 1, 1))

    def opp_direct(i):
        return remote(opp.at[i], relay_in.at[i], rel_s.at[i], rel_r.at[i], peer(0, 0, 1))

    def cross_copy(dg, i):
        return remote(cross.at[dg, i], cross_in.at[dg, i], crs_s.at[dg, i], crs_r.at[dg, i], peer(dg, 1, 1))

    def own_rows(ii):
        def one(n, carry):
            @pl.when(jnp.logical_and(ii == 0, n == 1))
            def _():
                a_copy(2).start()
                b_copy(2).start()

            @pl.when(jnp.logical_and(ii == 0, n == 3))
            def _():
                pass_on(2, 0)
                for which in range(2):
                    via_copy(1, 1, which).start()
                a_copy(3).start()
                b_copy(3).start()

            spectrum(keep, other, 4 * ii + n, pl.multiple_of(128 * n, 128), 512)
            return carry

        lax.fori_loop(0, 4, one, 0)
        for dh in (1, 0):
            for dg in range(2):
                total = dot(ww[...], spec[block_at(dg, dh)])
                if dh == 0:
                    near[dg, ii] = total[0:256]
                else:
                    side[dg, ii] = total[0:256]
                    for n in (1, 3):
                        row_copy(dg, 4 * ii + n).start()
                pp[2 * dg + dh, ii] = total[256:512]
        near_copy(ii).start()

    def collect(i):
        n, ii = lax.rem(i, 4), i // 4
        at = dest_rows(n)
        for dg in range(2):
            cross_copy(dg, i).wait()
        parts = [
            near[0, ii, at, :] + side_in[0, ii, at, :] + cross_in[0, i],
            near_in[ii, at, :] + side_in[1, ii, at, :] + cross_in[1, i],
        ]
        got = dot(jnp.concatenate(split(jnp.concatenate(parts, axis=0)), axis=0), perm[h])
        rows = got[0:128] + got[128:256]
        for dg in range(2):
            row = 4 * (3 - block_of(n)) + 2 * lax.rem(g + dg, 2) + ii
            for c in range(4):
                for part in range(2):
                    at = 64 * dg + 32 * part
                    flat[c, part, pl.ds(row, 32, stride=16), :] = rows[at : at + 32, 128 * c : 128 * c + 128]

    def relay(i):
        n, ii = lax.rem(i, 4), i // 4

        @pl.when(lax.rem(i, 2) == 0)
        def _():
            opp_cross(i).wait()
            at = dest_rows(n)
            for dg in range(2):
                side[dg, ii, at, :] = side[dg, ii, at, :] + relay_in[i, dg]
                row_copy(dg, i).start()

        @pl.when(lax.rem(i, 2) == 1)
        def _():
            opp_direct(i).wait()
            for dg in range(2):
                cross[dg, i] = cross[dg, i] + relay_in[i, dg]
                cross_copy(dg, i).start()

    def step(i, carry):
        n, ii = lax.rem(i, 4), i // 4

        @pl.when(i == 1)
        def _():
            a_copy(5).start()
            b_copy(5).start()

        @pl.when(i == 2)
        def _():
            pass_on(3, 0)
            a_copy(6).start()
            b_copy(6).start()

        @pl.when(i == 3)
        def _():
            pass_on(2, 1)

        @pl.when(i == 5)
        def _():
            pass_on(3, 1)

        @pl.when(jnp.logical_or(i == 0, i == 3))
        def _():
            own_rows(i // 3)

        a_copy(i).wait_recv()
        b_copy(i).wait_recv()

        spectrum(halo_a, halo_b, i, 0, 128)
        mine = pl.ds(pl.multiple_of(64 * n, 64), 64)
        for dh in range(2):
            for dg in range(2):
                total = dot(wh[n], spec[block_at(dg, dh), 0:384, :])
                pp[2 * dg + dh, ii] = pp[2 * dg + dh, ii] + total
                if dh == 0:
                    opp[i, dg] = pp[2 * dg, ii, mine, :]
                else:
                    cross[dg, i] = pp[2 * dg + 1, ii, mine, :]
            if dh == 0:

                @pl.when(lax.rem(i, 2) == 0)
                def _():
                    opp_cross(i).start()

                @pl.when(lax.rem(i, 2) == 1)
                def _():
                    opp_direct(i).start()

        @pl.when(lax.rem(i, 2) == 0)
        def _():
            for dg in range(2):
                cross_copy(dg, i).start()

        @pl.when(i >= 1)
        def _():
            relay(i - 1)

        @pl.when(i >= 4)
        def _():
            @pl.when(i == 4)
            def _():
                near_copy(0).wait()

            for dg in range(2):
                row_copy(dg, i - 4).wait()
            collect(i - 4)

        return carry

    lax.fori_loop(0, 8, step, 0)
    relay(7)
    near_copy(1).wait()

    def last(i, carry):
        for dg in range(2):
            row_copy(dg, i).wait()
        collect(i)
        return carry

    lax.fori_loop(4, 8, last, 0)
    results = [
        pltpu.make_async_copy(flat.at[c], out.at[:, :, pl.ds(128 * c, 128)], load_sem.at[c]) for c in range(4)
    ]
    for c in results:
        c.start()
    for i in range(8):
        snd_copy(i).wait_send()
        if i not in (4, 7):
            a_copy(i).wait_send()
            b_copy(i).wait_send()
    for hops in range(1, 4):
        for k in range(2):
            for which in range(2):
                via_copy(hops, k, which).wait_send()
    for c in results:
        c.wait()


def local(strips, field, spectral_phase, chirp_shift, tile_map, tile_phase):
    waves, tw = dft_tables()
    vmem = pl.BlockSpec(memory_space=pltpu.VMEM)
    hbm = pl.BlockSpec(memory_space=pl.ANY)
    rows = pltpu.VMEM((8, 2, 32, 1024), F32)
    small = pltpu.VMEM((16, 128), F32)
    phase = pltpu.VMEM((2, 32, NY), F32)
    sums = pltpu.VMEM((2, 2, 256, 512), F32)
    dma = pltpu.SemaphoreType.DMA
    out = pl.pallas_call(
        functools.partial(kernel, strips),
        in_specs=[hbm, hbm, hbm, hbm, vmem, vmem, pl.BlockSpec(memory_space=pltpu.SMEM)],
        out_specs=pl.BlockSpec(memory_space=pl.ANY),
        out_shape=jax.ShapeDtypeStruct((2, 512, 512), F32),
        scratch_shapes=[
            pltpu.VMEM((8, 2, 512, 128), F32),
            rows, rows, rows, rows, rows,
            small, small, small, small,
            pltpu.VMEM((32, NY), F32),
            pltpu.VMEM(waves.shape, F32),
            pltpu.VMEM(tw.shape, F32),
            phase, phase,
            pltpu.VMEM((2, 1536, 512), BF),
            pltpu.VMEM((2, 512, 512), BF),
            pltpu.VMEM((512, 1536), BF),
            pltpu.VMEM((4, 256, 384), BF),
            pltpu.VMEM((2, 256, 1536), BF),
            pltpu.VMEM((4, 1536, 512), BF),
            sums,
            pltpu.VMEM((2, 256, 512), F32),
            sums, sums,
            pltpu.VMEM((4, 2, 256, 512), F32),
            pltpu.VMEM((8, 2, 64, 512), F32),
            pltpu.VMEM((8, 2, 64, 512), F32),
            pltpu.VMEM((2, 8, 64, 512), F32),
            pltpu.VMEM((2, 8, 64, 512), F32),
            pltpu.VMEM((2, 2, 2, 32, 1024), F32),
            pltpu.VMEM((2, 2, 2, 32, 1024), F32),
            dma((11,)),
            *[dma((8,))] * 6,
            dma((3,)), dma((3,)),
            dma((2,)), dma((2,)),
            dma((2, 8)), dma((2, 8)),
            dma((8,)), dma((8,)),
            dma((2, 8)), dma((2, 8)),
            *[dma((2, 2))] * 4,
        ],
        compiler_params=pltpu.CompilerParams(
            collective_id=0, has_side_effects=True, vmem_limit_bytes=VMEM * 2**20
        ),
        cost_estimate=pl.CostEstimate(flops=40 * 10**9, bytes_accessed=10 * 2**20, transcendentals=0),
    )(
        field.reshape(2, 512, 1024), spectral_phase, jnp.asarray(waves), jnp.asarray(tw),
        chirp_shift.reshape(1, 32), tile_phase, tile_map,
    )
    return out.reshape(2, NT, 16, 512)


def solution(mesh):
    placed = (P(None, "freq", "xs", "yh"), P("freq", None), P("freq"), P("xs"), P(None, "freq"))
    return jax.shard_map(
        functools.partial(local, mesh.shape["xs"]),
        mesh=mesh,
        in_specs=placed,
        out_specs=P(None, None, "xs", ("freq", "yh")),
        check_vma=False,
    )
```

profile of v0, /device:TPU:1, one launch (start us, length us, event | category | flops | bytes accessed | tf_op | source)
XLA Modules:
  0.0 114.4 jit_solution(509889272223656090)
XLA Ops:
  0.0 111.2 %shard_map.73 = f32[2,512,512]{2,1,0:T(8,128)} custom-call(f32[2,512,1024]{2,1,0:T(8,128)} %bitcast.4, f32[32,2048]{1,0:T(8,128)} %phi_hbm.1, f32[2,2,256,256]{3,2,1,0:T(8,128)} %constant.4.clone.waves_hbm, f32[2,8,256]{2,1,0:T(8,128)} %constant.5.clone.tw_hbm, s32[1,32]{1,0:T(1,128)} %bitcast.5, f32[4,32]{1,0:T(4,128)} %tile_phase.1, s32[4]{0:T(128)} %tile_ids.1), custom_call_target="tpu_custom_call" | custom-call | flops 40000000000 | bytes 10485760 | tf_op jit(solution)/shard_map/pallas_call | solution.py:519
  111.2 3.2 %copy.9 = f32[2,32,16,512]{3,2,1,0:T(8,128)} copy(f32[2,32,16,512]{3,2,1,0:T(8,128)} %bitcast.3) | data formatting | bytes 4194304
where the time goes:
time: 115 us; the launch traced here: 114 us
  Pallas kernels  111 us (97%)
  local copies, waits for them, and re-layouts  3.22 us (3%)
    pallas_call x1, Pallas kernels, local(): pl.pallas_call(functools.partial(kernel, strips), in_specs=[hbm, hbm, hbm...  111 us
    unnamed x1, local copies, waits for them, and re-layouts  3.22 us

commit v1 on v0

--- a/solution.py
+++ b/solution.py
@@ -152,7 +152,7 @@
         return remote(other.at[i], halo_b.at[i], hb_s.at[i], hb_r.at[i], (g, onward, h))
 
     def via_copy(hops, k, which):
-        i = 4 + 3 * k
+        i = 4 + 2 * k
         if hops == 1:
             src = (keep, other)[which].at[i]
             return remote(src, via_1.at[k, which], v1_s.at[k, which], v1_r.at[k, which], (g, across, h))
@@ -196,23 +196,20 @@
         gather_rows(i, g, keep)
         return carry
 
-    for i in (0, 4, 1):
+    for i in (0, 4):
         gather_rows(i, g, keep)
     pl.semaphore_wait(barrier, len(greet))
     a_copy(0).start()
     via_copy(1, 0, 0).start()
-    a_copy(1).start()
     lax.fori_loop(0, 8, pack_send, 0)
     prm_core.start()
     prm_strip.start()
-    lax.fori_loop(2, 4, pack_keep, 0)
+    lax.fori_loop(1, 4, pack_keep, 0)
     lax.fori_loop(5, 8, pack_keep, 0)
-    for i in (0, 4, 1):
-        snd_copy(i).wait_recv()
-        if i == 4:
-            via_copy(1, 0, 1).start()
-        else:
-            b_copy(i).start()
+    snd_copy(0).wait_recv()
+    b_copy(0).start()
+    snd_copy(4).wait_recv()
+    via_copy(1, 0, 1).start()
 
     for c in tables:
         c.wait()
@@ -286,9 +283,13 @@
                 ww[rows, at : at + 128] = u
                 ww[below, at : at + 128] = v
                 wh[n, rows, 128 * k : 128 * k + 128] = w
-    for i in (2, 3, 5, 6, 7):
+    for i in (1, 2, 3, 5, 6, 7):
         snd_copy(i).wait_recv()
     e_copy.wait()
+    a_copy(1).start()
+    b_copy(1).start()
+    for which in range(2):
+        via_copy(1, 1, which).start()
 
     def spectrum(a, b, i, at, depth):
         re = jnp.concatenate([a[i, 0], b[i, 0]], axis=0)
@@ -343,18 +344,11 @@
 
     def own_rows(ii):
         def one(n, carry):
-            @pl.when(jnp.logical_and(ii == 0, n == 1))
-            def _():
-                a_copy(2).start()
-                b_copy(2).start()
-
             @pl.when(jnp.logical_and(ii == 0, n == 3))
             def _():
                 pass_on(2, 0)
-                for which in range(2):
-                    via_copy(1, 1, which).start()
-                a_copy(3).start()
-                b_copy(3).start()
+                a_copy(2).start()
+                b_copy(2).start()
 
             spectrum(keep, other, 4 * ii + n, pl.multiple_of(128 * n, 128), 512)
             return carry
@@ -411,20 +405,17 @@
     def step(i, carry):
         n, ii = lax.rem(i, 4), i // 4
 
-        @pl.when(i == 1)
-        def _():
-            a_copy(5).start()
-            b_copy(5).start()
+        for now, start in ((2, 3), (3, 5), (4, 7)):
+
+            @pl.when(i == now)
+            def _():
+                a_copy(start).start()
+                b_copy(start).start()
 
         @pl.when(i == 2)
         def _():
+            pass_on(2, 1)
             pass_on(3, 0)
-            a_copy(6).start()
-            b_copy(6).start()
-
-        @pl.when(i == 3)
-        def _():
-            pass_on(2, 1)
 
         @pl.when(i == 5)
         def _():
@@ -479,7 +470,6 @@
         return carry
 
     lax.fori_loop(0, 8, step, 0)
-    relay(7)
     near_copy(1).wait()
 
     def last(i, carry):
@@ -488,7 +478,9 @@
         collect(i)
         return carry
 
-    lax.fori_loop(4, 8, last, 0)
+    lax.fori_loop(4, 6, last, 0)
+    relay(7)
+    lax.fori_loop(6, 8, last, 0)
     results = [
         pltpu.make_async_copy(flat.at[c], out.at[:, :, pl.ds(128 * c, 128)], load_sem.at[c]) for c in range(4)
     ]
@@ -496,7 +488,7 @@
         c.start()
     for i in range(8):
         snd_copy(i).wait_send()
-        if i not in (4, 7):
+        if i not in (4, 6):
             a_copy(i).wait_send()
             b_copy(i).wait_send()
     for hops in range(1, 4):

time: 115 us -> 127 us (1.10)
  Pallas kernels: 111 us -> 124 us
    pallas_call x1, Pallas kernels: 111 us -> 124 us  [local(): pl.pallas_call(functools.partial(kernel, strips), in_specs=[hbm, hbm, hbm...]
where the time goes in v1:
time: 127 us
  Pallas kernels  124 us (98%)
  local copies, waits for them, and re-layouts  3.22 us (3%)
    pallas_call x1, Pallas kernels, local(): pl.pallas_call(functools.partial(kernel, strips), in_specs=[hbm, hbm, hbm...  124 us
    unnamed x1, local copies, waits for them, and re-layouts  3.22 us

profile of v1, /device:TPU:1, one launch (start us, length us, event | category | flops | bytes accessed | tf_op | source)
XLA Modules:
  0.0 127.1 jit_solution(1465523275872554023)
XLA Ops:
  0.0 123.8 %shard_map.73 = f32[2,512,512]{2,1,0:T(8,128)} custom-call(f32[2,512,1024]{2,1,0:T(8,128)} %bitcast.4, f32[32,2048]{1,0:T(8,128)} %phi_hbm.1, f32[2,2,256,256]{3,2,1,0:T(8,128)} %constant.4.clone.waves_hbm, f32[2,8,256]{2,1,0:T(8,128)} %constant.5.clone.tw_hbm, s32[1,32]{1,0:T(1,128)} %bitcast.5, f32[4,32]{1,0:T(4,128)} %tile_phase.1, s32[4]{0:T(128)} %tile_ids.1), custom_call_target="tpu_custom_call" | custom-call | flops 40000000000 | bytes 10485760 | tf_op jit(solution)/shard_map/pallas_call | solution.py:511
  123.8 3.2 %copy.9 = f32[2,32,16,512]{3,2,1,0:T(8,128)} copy(f32[2,32,16,512]{3,2,1,0:T(8,128)} %bitcast.3) | data formatting | bytes 4194304

commit v2 on v0

--- a/solution.py
+++ b/solution.py
@@ -151,22 +151,22 @@
     def b_copy(i):
         return remote(other.at[i], halo_b.at[i], hb_s.at[i], hb_r.at[i], (g, onward, h))
 
-    def via_copy(hops, k, which):
-        i = 4 + 3 * k
+    def via_copy(hops, which):
+        i = 4
         if hops == 1:
             src = (keep, other)[which].at[i]
-            return remote(src, via_1.at[k, which], v1_s.at[k, which], v1_r.at[k, which], (g, across, h))
+            return remote(src, via_1.at[which], v1_s.at[which], v1_r.at[which], (g, across, h))
         if hops == 2:
             return remote(
-                via_1.at[k, which], via_2.at[k, which], v2_s.at[k, which], v2_r.at[k, which], (g, across, h)
+                via_1.at[which], via_2.at[which], v2_s.at[which], v2_r.at[which], (g, across, h)
             )
         dst, sems = ((halo_a, (ha_s, ha_r)), (halo_b, (hb_s, hb_r)))[which]
-        return remote(via_2.at[k, which], dst.at[i], sems[0].at[i], sems[1].at[i], (g, third, h))
-
-    def pass_on(hops, k):
+        return remote(via_2.at[which], dst.at[i], sems[0].at[i], sems[1].at[i], (g, third, h))
+
+    def pass_on(hops):
         for which in range(2):
-            via_copy(hops - 1, k, which).wait_recv()
-            via_copy(hops, k, which).start()
+            via_copy(hops - 1, which).wait_recv()
+            via_copy(hops, which).start()
 
     def gather_rows(i, whose, into):
         row = 4 * block_of(lax.rem(i, 4)) + 2 * whose + i // 4
@@ -200,7 +200,7 @@
         gather_rows(i, g, keep)
     pl.semaphore_wait(barrier, len(greet))
     a_copy(0).start()
-    via_copy(1, 0, 0).start()
+    via_copy(1, 0).start()
     a_copy(1).start()
     lax.fori_loop(0, 8, pack_send, 0)
     prm_core.start()
@@ -210,7 +210,7 @@
     for i in (0, 4, 1):
         snd_copy(i).wait_recv()
         if i == 4:
-            via_copy(1, 0, 1).start()
+            via_copy(1, 1).start()
         else:
             b_copy(i).start()
 
@@ -350,9 +350,7 @@
 
             @pl.when(jnp.logical_and(ii == 0, n == 3))
             def _():
-                pass_on(2, 0)
-                for which in range(2):
-                    via_copy(1, 1, which).start()
+                pass_on(2)
                 a_copy(3).start()
                 b_copy(3).start()
 
@@ -418,17 +416,14 @@
 
         @pl.when(i == 2)
         def _():
-            pass_on(3, 0)
+            pass_on(3)
             a_copy(6).start()
             b_copy(6).start()
 
         @pl.when(i == 3)
         def _():
-            pass_on(2, 1)
-
-        @pl.when(i == 5)
-        def _():
-            pass_on(3, 1)
+            a_copy(7).start()
+            b_copy(7).start()
 
         @pl.when(jnp.logical_or(i == 0, i == 3))
         def _():
@@ -479,7 +474,6 @@
         return carry
 
     lax.fori_loop(0, 8, step, 0)
-    relay(7)
     near_copy(1).wait()
 
     def last(i, carry):
@@ -488,7 +482,9 @@
         collect(i)
         return carry
 
-    lax.fori_loop(4, 8, last, 0)
+    lax.fori_loop(4, 6, last, 0)
+    relay(7)
+    lax.fori_loop(6, 8, last, 0)
     results = [
         pltpu.make_async_copy(flat.at[c], out.at[:, :, pl.ds(128 * c, 128)], load_sem.at[c]) for c in range(4)
     ]
@@ -496,13 +492,12 @@
         c.start()
     for i in range(8):
         snd_copy(i).wait_send()
-        if i not in (4, 7):
+        if i != 4:
             a_copy(i).wait_send()
             b_copy(i).wait_send()
     for hops in range(1, 4):
-        for k in range(2):
-            for which in range(2):
-                via_copy(hops, k, which).wait_send()
+        for which in range(2):
+            via_copy(hops, which).wait_send()
     for c in results:
         c.wait()
 
@@ -543,8 +538,8 @@
             pltpu.VMEM((8, 2, 64, 512), F32),
             pltpu.VMEM((2, 8, 64, 512), F32),
             pltpu.VMEM((2, 8, 64, 512), F32),
-            pltpu.VMEM((2, 2, 2, 32, 1024), F32),
-            pltpu.VMEM((2, 2, 2, 32, 1024), F32),
+            pltpu.VMEM((2, 2, 32, 1024), F32),
+            pltpu.VMEM((2, 2, 32, 1024), F32),
             dma((11,)),
             *[dma((8,))] * 6,
             dma((3,)), dma((3,)),
@@ -552,7 +547,7 @@
             dma((2, 8)), dma((2, 8)),
             dma((8,)), dma((8,)),
             dma((2, 8)), dma((2, 8)),
-            *[dma((2, 2))] * 4,
+            *[dma((2,))] * 4,
         ],
         compiler_params=pltpu.CompilerParams(
             collective_id=0, has_side_effects=True, vmem_limit_bytes=VMEM * 2**20

time: 115 us -> 115 us (level)
  no operation moved by 1% of the time
where the time goes in v2:
time: 115 us
  Pallas kernels  112 us (97%)
  local copies, waits for them, and re-layouts  3.22 us (3%)
    pallas_call x1, Pallas kernels, local(): pl.pallas_call(functools.partial(kernel, strips), in_specs=[hbm, hbm, hbm...  112 us
    unnamed x1, local copies, waits for them, and re-layouts  3.22 us

profile of v2, /device:TPU:1, one launch (start us, length us, event | category | flops | bytes accessed | tf_op | source)
XLA Modules:
  0.0 115.3 jit_solution(3981847666367571120)
XLA Ops:
  0.0 112.1 %shard_map.73 = f32[2,512,512]{2,1,0:T(8,128)} custom-call(f32[2,512,1024]{2,1,0:T(8,128)} %bitcast.4, f32[32,2048]{1,0:T(8,128)} %phi_hbm.1, f32[2,2,256,256]{3,2,1,0:T(8,128)} %constant.4.clone.waves_hbm, f32[2,8,256]{2,1,0:T(8,128)} %constant.5.clone.tw_hbm, s32[1,32]{1,0:T(1,128)} %bitcast.5, f32[4,32]{1,0:T(4,128)} %tile_phase.1, s32[4]{0:T(128)} %tile_ids.1), custom_call_target="tpu_custom_call" | custom-call | flops 40000000000 | bytes 10485760 | tf_op jit(solution)/shard_map/pallas_call | solution.py:514
  112.1 3.2 %copy.9 = f32[2,32,16,512]{3,2,1,0:T(8,128)} copy(f32[2,32,16,512]{3,2,1,0:T(8,128)} %bitcast.3) | data formatting | bytes 4194304

commit v3 on v2

--- a/solution.py
+++ b/solution.py
@@ -151,22 +151,20 @@
     def b_copy(i):
         return remote(other.at[i], halo_b.at[i], hb_s.at[i], hb_r.at[i], (g, onward, h))
 
-    def via_copy(hops, which):
-        i = 4
+    def via_copy(hops, slot):
+        which, i = ((0, 4), (1, 4), (1, 6))[slot]
         if hops == 1:
             src = (keep, other)[which].at[i]
-            return remote(src, via_1.at[which], v1_s.at[which], v1_r.at[which], (g, across, h))
+            return remote(src, via_1.at[slot], v1_s.at[slot], v1_r.at[slot], (g, across, h))
         if hops == 2:
-            return remote(
-                via_1.at[which], via_2.at[which], v2_s.at[which], v2_r.at[which], (g, across, h)
-            )
+            return remote(via_1.at[slot], via_2.at[slot], v2_s.at[slot], v2_r.at[slot], (g, across, h))
         dst, sems = ((halo_a, (ha_s, ha_r)), (halo_b, (hb_s, hb_r)))[which]
-        return remote(via_2.at[which], dst.at[i], sems[0].at[i], sems[1].at[i], (g, third, h))
-
-    def pass_on(hops):
-        for which in range(2):
-            via_copy(hops - 1, which).wait_recv()
-            via_copy(hops, which).start()
+        return remote(via_2.at[slot], dst.at[i], sems[0].at[i], sems[1].at[i], (g, third, h))
+
+    def pass_on(hops, slots):
+        for slot in slots:
+            via_copy(hops - 1, slot).wait_recv()
+            via_copy(hops, slot).start()
 
     def gather_rows(i, whose, into):
         row = 4 * block_of(lax.rem(i, 4)) + 2 * whose + i // 4
@@ -289,6 +287,7 @@
     for i in (2, 3, 5, 6, 7):
         snd_copy(i).wait_recv()
     e_copy.wait()
+    via_copy(1, 2).start()
 
     def spectrum(a, b, i, at, depth):
         re = jnp.concatenate([a[i, 0], b[i, 0]], axis=0)
@@ -332,11 +331,14 @@
         at, ii = dest_rows(lax.rem(i, 4)), i // 4
         return remote(side.at[dg, ii, at], side_in.at[dg, ii, at], row_s.at[dg, i], row_r.at[dg, i], peer(dg, 0, 1))
 
-    def opp_cross(i):
-        return remote(opp.at[i], relay_in.at[i], rel_s.at[i], rel_r.at[i], peer(0, 1, 1))
-
-    def opp_direct(i):
-        return remote(opp.at[i], relay_in.at[i], rel_s.at[i], rel_r.at[i], peer(0, 0, 1))
+    def opp_copy(dg, i, to):
+        return remote(opp.at[i, dg], relay_in.at[i, dg], rel_s.at[i, dg], rel_r.at[i, dg], to)
+
+    def opp_cross(dg, i):
+        return opp_copy(dg, i, peer(0, 1, 1))
+
+    def opp_direct(dg, i):
+        return opp_copy(dg, i, peer(0, 0, 1))
 
     def cross_copy(dg, i):
         return remote(cross.at[dg, i], cross_in.at[dg, i], crs_s.at[dg, i], crs_r.at[dg, i], peer(dg, 1, 1))
@@ -350,7 +352,7 @@
 
             @pl.when(jnp.logical_and(ii == 0, n == 3))
             def _():
-                pass_on(2)
+                pass_on(2, (0, 1))
                 a_copy(3).start()
                 b_copy(3).start()
 
@@ -393,16 +395,16 @@
 
         @pl.when(lax.rem(i, 2) == 0)
         def _():
-            opp_cross(i).wait()
             at = dest_rows(n)
             for dg in range(2):
+                opp_cross(dg, i).wait()
                 side[dg, ii, at, :] = side[dg, ii, at, :] + relay_in[i, dg]
                 row_copy(dg, i).start()
 
         @pl.when(lax.rem(i, 2) == 1)
         def _():
-            opp_direct(i).wait()
             for dg in range(2):
+                opp_direct(dg, i).wait()
                 cross[dg, i] = cross[dg, i] + relay_in[i, dg]
                 cross_copy(dg, i).start()
 
@@ -416,14 +418,18 @@
 
         @pl.when(i == 2)
         def _():
-            pass_on(3)
+            pass_on(3, (0, 1))
             a_copy(6).start()
-            b_copy(6).start()
 
         @pl.when(i == 3)
         def _():
             a_copy(7).start()
             b_copy(7).start()
+            pass_on(2, (2,))
+
+        @pl.when(i == 4)
+        def _():
+            pass_on(3, (2,))
 
         @pl.when(jnp.logical_or(i == 0, i == 3))
         def _():
@@ -438,19 +444,18 @@
             for dg in range(2):
                 total = dot(wh[n], spec[block_at(dg, dh), 0:384, :])
                 pp[2 * dg + dh, ii] = pp[2 * dg + dh, ii] + total
-                if dh == 0:
-                    opp[i, dg] = pp[2 * dg, ii, mine, :]
-                else:
+                if dh == 1:
                     cross[dg, i] = pp[2 * dg + 1, ii, mine, :]
-            if dh == 0:
+                    continue
+                opp[i, dg] = pp[2 * dg, ii, mine, :]
 
                 @pl.when(lax.rem(i, 2) == 0)
                 def _():
-                    opp_cross(i).start()
+                    opp_cross(dg, i).start()
 
                 @pl.when(lax.rem(i, 2) == 1)
                 def _():
-                    opp_direct(i).start()
+                    opp_direct(dg, i).start()
 
         @pl.when(lax.rem(i, 2) == 0)
         def _():
@@ -494,10 +499,11 @@
         snd_copy(i).wait_send()
         if i != 4:
             a_copy(i).wait_send()
+        if i not in (4, 6):
             b_copy(i).wait_send()
     for hops in range(1, 4):
-        for which in range(2):
-            via_copy(hops, which).wait_send()
+        for slot in range(3):
+            via_copy(hops, slot).wait_send()
     for c in results:
         c.wait()
 
@@ -538,16 +544,16 @@
             pltpu.VMEM((8, 2, 64, 512), F32),
             pltpu.VMEM((2, 8, 64, 512), F32),
             pltpu.VMEM((2, 8, 64, 512), F32),
-            pltpu.VMEM((2, 2, 32, 1024), F32),
-            pltpu.VMEM((2, 2, 32, 1024), F32),
+            pltpu.VMEM((3, 2, 32, 1024), F32),
+            pltpu.VMEM((3, 2, 32, 1024), F32),
             dma((11,)),
             *[dma((8,))] * 6,
             dma((3,)), dma((3,)),
             dma((2,)), dma((2,)),
             dma((2, 8)), dma((2, 8)),
-            dma((8,)), dma((8,)),
+            dma((8, 2)), dma((8, 2)),
             dma((2, 8)), dma((2, 8)),
-            *[dma((2,))] * 4,
+            *[dma((3,))] * 4,
         ],
         compiler_params=pltpu.CompilerParams(
             collective_id=0, has_side_effects=True, vmem_limit_bytes=VMEM * 2**20

time: 115 us -> 116 us (level); the launches traced: 115 us -> 115 us
  no operation moved by 1% of the time
where the time goes in v3:
time: 116 us; the launch traced here: 115 us
  Pallas kernels  111 us (96%)
  local copies, waits for them, and re-layouts  3.22 us (3%)
    pallas_call x1, Pallas kernels, local(): pl.pallas_call(functools.partial(kernel, strips), in_specs=[hbm, hbm, hbm...  111 us
    unnamed x1, local copies, waits for them, and re-layouts  3.22 us

profile of v3, /device:TPU:1, one launch (start us, length us, event | category | flops | bytes accessed | tf_op | source)
XLA Modules:
  0.0 114.7 jit_solution(2796381604732976122)
XLA Ops:
  0.0 111.5 %shard_map.73 = f32[2,512,512]{2,1,0:T(8,128)} custom-call(f32[2,512,1024]{2,1,0:T(8,128)} %bitcast.4, f32[32,2048]{1,0:T(8,128)} %phi_hbm.1, f32[2,2,256,256]{3,2,1,0:T(8,128)} %constant.4.clone.waves_hbm, f32[2,8,256]{2,1,0:T(8,128)} %constant.5.clone.tw_hbm, s32[1,32]{1,0:T(1,128)} %bitcast.5, f32[4,32]{1,0:T(4,128)} %tile_phase.1, s32[4]{0:T(128)} %tile_ids.1), custom_call_target="tpu_custom_call" | custom-call | flops 40000000000 | bytes 10485760 | tf_op jit(solution)/shard_map/pallas_call | solution.py:520
  111.5 3.2 %copy.9 = f32[2,32,16,512]{3,2,1,0:T(8,128)} copy(f32[2,32,16,512]{3,2,1,0:T(8,128)} %bitcast.3) | data formatting | bytes 4194304

commit v4 on v3

--- a/solution.py
+++ b/solution.py
@@ -152,7 +152,7 @@
         return remote(other.at[i], halo_b.at[i], hb_s.at[i], hb_r.at[i], (g, onward, h))
 
     def via_copy(hops, slot):
-        which, i = ((0, 4), (1, 4), (1, 6))[slot]
+        which, i = ((0, 4), (1, 4))[slot]
         if hops == 1:
             src = (keep, other)[which].at[i]
             return remote(src, via_1.at[slot], v1_s.at[slot], v1_r.at[slot], (g, across, h))
@@ -287,7 +287,6 @@
     for i in (2, 3, 5, 6, 7):
         snd_copy(i).wait_recv()
     e_copy.wait()
-    via_copy(1, 2).start()
 
     def spectrum(a, b, i, at, depth):
         re = jnp.concatenate([a[i, 0], b[i, 0]], axis=0)
@@ -367,8 +366,12 @@
                     near[dg, ii] = total[0:256]
                 else:
                     side[dg, ii] = total[0:256]
-                    for n in (1, 3):
-                        row_copy(dg, 4 * ii + n).start()
+                    row_copy(dg, 4 * ii + 1).start()
+
+                    @pl.when(ii == 0)
+                    def _():
+                        row_copy(dg, 3).start()
+
                 pp[2 * dg + dh, ii] = total[256:512]
         near_copy(ii).start()
 
@@ -420,20 +423,16 @@
         def _():
             pass_on(3, (0, 1))
             a_copy(6).start()
+            b_copy(6).start()
 
         @pl.when(i == 3)
         def _():
             a_copy(7).start()
             b_copy(7).start()
-            pass_on(2, (2,))
-
-        @pl.when(i == 4)
-        def _():
-            pass_on(3, (2,))
-
-        @pl.when(jnp.logical_or(i == 0, i == 3))
-        def _():
-            own_rows(i // 3)
+
+        @pl.when(i < 2)
+        def _():
+            own_rows(i)
 
         a_copy(i).wait_recv()
         b_copy(i).wait_recv()
@@ -465,6 +464,11 @@
         @pl.when(i >= 1)
         def _():
             relay(i - 1)
+
+        @pl.when(i == 3)
+        def _():
+            for dg in range(2):
+                row_copy(dg, 7).start()
 
         @pl.when(i >= 4)
         def _():
@@ -499,10 +503,10 @@
         snd_copy(i).wait_send()
         if i != 4:
             a_copy(i).wait_send()
-        if i not in (4, 6):
+        if i != 4:
             b_copy(i).wait_send()
     for hops in range(1, 4):
-        for slot in range(3):
+        for slot in range(2):
             via_copy(hops, slot).wait_send()
     for c in results:
         c.wait()
@@ -544,8 +548,8 @@
             pltpu.VMEM((8, 2, 64, 512), F32),
             pltpu.VMEM((2, 8, 64, 512), F32),
             pltpu.VMEM((2, 8, 64, 512), F32),
-            pltpu.VMEM((3, 2, 32, 1024), F32),
-            pltpu.VMEM((3, 2, 32, 1024), F32),
+            pltpu.VMEM((2, 2, 32, 1024), F32),
+            pltpu.VMEM((2, 2, 32, 1024), F32),
             dma((11,)),
             *[dma((8,))] * 6,
             dma((3,)), dma((3,)),
@@ -553,7 +557,7 @@
             dma((2, 8)), dma((2, 8)),
             dma((8, 2)), dma((8, 2)),
             dma((2, 8)), dma((2, 8)),
-            *[dma((3,))] * 4,
+            *[dma((2,))] * 4,
         ],
         compiler_params=pltpu.CompilerParams(
             collective_id=0, has_side_effects=True, vmem_limit_bytes=VMEM * 2**20

time: 116 us -> 115 us (level)
  no operation moved by 1% of the time
where the time goes in v4:
time: 115 us
  Pallas kernels  111 us (97%)
  local copies, waits for them, and re-layouts  3.22 us (3%)
    pallas_call x1, Pallas kernels, local(): pl.pallas_call(functools.partial(kernel, strips), in_specs=[hbm, hbm, hbm...  111 us
    unnamed x1, local copies, waits for them, and re-layouts  3.22 us

profile of v4, /device:TPU:1, one launch (start us, length us, event | category | flops | bytes accessed | tf_op | source)
XLA Modules:
  0.0 114.7 jit_solution(8898453542862471030)
XLA Ops:
  0.0 111.4 %shard_map.73 = f32[2,512,512]{2,1,0:T(8,128)} custom-call(f32[2,512,1024]{2,1,0:T(8,128)} %bitcast.4, f32[32,2048]{1,0:T(8,128)} %phi_hbm.1, f32[2,2,256,256]{3,2,1,0:T(8,128)} %constant.4.clone.waves_hbm, f32[2,8,256]{2,1,0:T(8,128)} %constant.5.clone.tw_hbm, s32[1,32]{1,0:T(1,128)} %bitcast.5, f32[4,32]{1,0:T(4,128)} %tile_phase.1, s32[4]{0:T(128)} %tile_ids.1), custom_call_target="tpu_custom_call" | custom-call | flops 40000000000 | bytes 10485760 | tf_op jit(solution)/shard_map/pallas_call | solution.py:524
  111.4 3.2 %copy.9 = f32[2,32,16,512]{3,2,1,0:T(8,128)} copy(f32[2,32,16,512]{3,2,1,0:T(8,128)} %bitcast.3) | data formatting | bytes 4194304

commit v5 on v4

--- a/solution.py
+++ b/solution.py
@@ -200,11 +200,10 @@
     a_copy(0).start()
     via_copy(1, 0).start()
     a_copy(1).start()
-    lax.fori_loop(0, 8, pack_send, 0)
+    lax.fori_loop(0, 5, pack_send, 0)
     prm_core.start()
     prm_strip.start()
     lax.fori_loop(2, 4, pack_keep, 0)
-    lax.fori_loop(5, 8, pack_keep, 0)
     for i in (0, 4, 1):
         snd_copy(i).wait_recv()
         if i == 4:
@@ -284,7 +283,7 @@
                 ww[rows, at : at + 128] = u
                 ww[below, at : at + 128] = v
                 wh[n, rows, 128 * k : 128 * k + 128] = w
-    for i in (2, 3, 5, 6, 7):
+    for i in (2, 3):
         snd_copy(i).wait_recv()
     e_copy.wait()
 
@@ -416,7 +415,11 @@
 
         @pl.when(i == 1)
         def _():
+            lax.fori_loop(5, 8, pack_send, 0)
+            lax.fori_loop(5, 8, pack_keep, 0)
             a_copy(5).start()
+            for late in range(5, 8):
+                snd_copy(late).wait_recv()
             b_copy(5).start()
 
         @pl.when(i == 2)

time: 115 us -> 117 us (1.017)
  Pallas kernels: 111 us -> 113 us
    pallas_call x1, Pallas kernels: 111 us -> 113 us  [local(): pl.pallas_call(functools.partial(kernel, strips), in_specs=[hbm, hbm, hbm...]
where the time goes in v5:
time: 117 us
  Pallas kernels  113 us (97%)
  local copies, waits for them, and re-layouts  3.22 us (3%)
    pallas_call x1, Pallas kernels, local(): pl.pallas_call(functools.partial(kernel, strips), in_specs=[hbm, hbm, hbm...  113 us
    unnamed x1, local copies, waits for them, and re-layouts  3.22 us

profile of v5, /device:TPU:1, one launch (start us, length us, event | category | flops | bytes accessed | tf_op | source)
XLA Modules:
  0.0 116.7 jit_solution(3584044942695902596)
XLA Ops:
  0.0 113.5 %shard_map.73 = f32[2,512,512]{2,1,0:T(8,128)} custom-call(f32[2,512,1024]{2,1,0:T(8,128)} %bitcast.4, f32[32,2048]{1,0:T(8,128)} %phi_hbm.1, f32[2,2,256,256]{3,2,1,0:T(8,128)} %constant.4.clone.waves_hbm, f32[2,8,256]{2,1,0:T(8,128)} %constant.5.clone.tw_hbm, s32[1,32]{1,0:T(1,128)} %bitcast.5, f32[4,32]{1,0:T(4,128)} %tile_phase.1, s32[4]{0:T(128)} %tile_ids.1), custom_call_target="tpu_custom_call" | custom-call | flops 40000000000 | bytes 10485760 | tf_op jit(solution)/shard_map/pallas_call | solution.py:527
  113.5 3.2 %copy.9 = f32[2,32,16,512]{3,2,1,0:T(8,128)} copy(f32[2,32,16,512]{3,2,1,0:T(8,128)} %bitcast.3) | data formatting | bytes 4194304

commit v6 on v4

--- a/solution.py
+++ b/solution.py
@@ -288,17 +288,21 @@
         snd_copy(i).wait_recv()
     e_copy.wait()
 
-    def spectrum(a, b, i, at, depth):
+    def spread_out(k, a, b, i):
         re = jnp.concatenate([a[i, 0], b[i, 0]], axis=0)
         im = jnp.concatenate([a[i, 1], b[i, 1]], axis=0)
         for half_p, parts in enumerate(butterflies(re, im, tw)):
             for j, pieces in enumerate(parts):
                 for half, w in enumerate(pieces):
                     hi, lo = split(w)
-                    for k, x in enumerate((hi, lo, hi)):
-                        at_k = 512 * k + 256 * half
-                        spread[half_p, 64 * j : 64 * j + 64, at_k : at_k + 256] = x
-        even, uneven = (dot(spread[k], table[k]) for k in range(2))
+                    for third, x in enumerate((hi, lo, hi)):
+                        at = 512 * third + 256 * half
+                        spread[k, half_p, 64 * j : 64 * j + 64, at : at + 256] = x
+
+    def transform(k):
+        return [dot(spread[k, p], table[p]) for p in range(2)]
+
+    def turn_phase(even, uneven, at, depth):
         early = lax.broadcasted_iota(jnp.int32, (64, 128), 1) < 64
         for j in range(4):
             for b4 in range(4):
@@ -343,22 +347,26 @@
         return remote(cross.at[dg, i], cross_in.at[dg, i], crs_s.at[dg, i], crs_r.at[dg, i], peer(dg, 1, 1))
 
     def own_rows(ii):
-        def one(n, carry):
-            @pl.when(jnp.logical_and(ii == 0, n == 1))
+        def two(m, carry):
+            @pl.when(jnp.logical_and(ii == 0, m == 0))
             def _():
                 a_copy(2).start()
                 b_copy(2).start()
 
-            @pl.when(jnp.logical_and(ii == 0, n == 3))
+            @pl.when(jnp.logical_and(ii == 0, m == 1))
             def _():
                 pass_on(2, (0, 1))
                 a_copy(3).start()
                 b_copy(3).start()
 
-            spectrum(keep, other, 4 * ii + n, pl.multiple_of(128 * n, 128), 512)
+            i, at = 4 * ii + 2 * m, pl.multiple_of(256 * m, 256)
+            spread_out(0, keep, other, i)
+            spread_out(1, keep, other, i + 1)
+            turn_phase(*transform(0), at, 512)
+            turn_phase(*transform(1), at + 128, 512)
             return carry
 
-        lax.fori_loop(0, 4, one, 0)
+        lax.fori_loop(0, 2, two, 0)
         for dh in (1, 0):
             for dg in range(2):
                 total = dot(ww[...], spec[block_at(dg, dh)])
@@ -437,29 +445,28 @@
         a_copy(i).wait_recv()
         b_copy(i).wait_recv()
 
-        spectrum(halo_a, halo_b, i, 0, 128)
-        mine = pl.ds(pl.multiple_of(64 * n, 64), 64)
-        for dh in range(2):
-            for dg in range(2):
-                total = dot(wh[n], spec[block_at(dg, dh), 0:384, :])
-                pp[2 * dg + dh, ii] = pp[2 * dg + dh, ii] + total
-                if dh == 1:
-                    cross[dg, i] = pp[2 * dg + 1, ii, mine, :]
-                    continue
-                opp[i, dg] = pp[2 * dg, ii, mine, :]
-
-                @pl.when(lax.rem(i, 2) == 0)
-                def _():
-                    opp_cross(dg, i).start()
-
-                @pl.when(lax.rem(i, 2) == 1)
-                def _():
-                    opp_direct(dg, i).start()
-
-        @pl.when(lax.rem(i, 2) == 0)
-        def _():
-            for dg in range(2):
-                cross_copy(dg, i).start()
+        spread_out(0, halo_a, halo_b, i)
+        turn_phase(*transform(0), 0, 128)
+        for nn in range(4):
+
+            @pl.when(n == nn)
+            def _():
+                rows = slice(64 * nn, 64 * nn + 64)
+                for dh in range(2):
+                    for dg in range(2):
+                        blk = 2 * dg + dh
+                        total = dot(wh[nn, 64 * nn :, :], spec[block_at(dg, dh), 0:384, :])
+                        value = pp[blk, ii, rows, :] + total[0:64]
+                        if nn < 3:
+                            pp[blk, ii, 64 * nn + 64 :, :] = pp[blk, ii, 64 * nn + 64 :, :] + total[64:]
+                        if dh == 1:
+                            cross[dg, i] = value
+                        else:
+                            opp[i, dg] = value
+                            (opp_direct if nn % 2 else opp_cross)(dg, i).start()
+                if nn % 2 == 0:
+                    for dg in range(2):
+                        cross_copy(dg, i).start()
 
         @pl.when(i >= 1)
         def _():
@@ -538,7 +545,7 @@
             pltpu.VMEM((2, 512, 512), BF),
             pltpu.VMEM((512, 1536), BF),
             pltpu.VMEM((4, 256, 384), BF),
-            pltpu.VMEM((2, 256, 1536), BF),
+            pltpu.VMEM((2, 2, 256, 1536), BF),
             pltpu.VMEM((4, 1536, 512), BF),
             sums,
             pltpu.VMEM((2, 256, 512), F32),

time: 115 us -> 115 us (level)
  no operation moved by 1% of the time
where the time goes in v6:
time: 115 us
  Pallas kernels  111 us (97%)
  local copies, waits for them, and re-layouts  3.22 us (3%)
    pallas_call x1, Pallas kernels, local(): pl.pallas_call(functools.partial(kernel, strips), in_specs=[hbm, hbm, hbm...  111 us
    unnamed x1, local copies, waits for them, and re-layouts  3.22 us

profile of v6, /device:TPU:1, one launch (start us, length us, event | category | flops | bytes accessed | tf_op | source)
XLA Modules:
  0.0 114.6 jit_solution(6351724694783634602)
XLA Ops:
  0.0 111.3 %shard_map.73 = f32[2,512,512]{2,1,0:T(8,128)} custom-call(f32[2,512,1024]{2,1,0:T(8,128)} %bitcast.4, f32[32,2048]{1,0:T(8,128)} %phi_hbm.1, f32[2,2,256,256]{3,2,1,0:T(8,128)} %constant.4.clone.waves_hbm, f32[2,8,256]{2,1,0:T(8,128)} %constant.5.clone.tw_hbm, s32[1,32]{1,0:T(1,128)} %bitcast.5, f32[4,32]{1,0:T(4,128)} %tile_phase.1, s32[4]{0:T(128)} %tile_ids.1), custom_call_target="tpu_custom_call" | custom-call | flops 40000000000 | bytes 10485760 | tf_op jit(solution)/shard_map/pallas_call | solution.py:531
  111.3 3.2 %copy.9 = f32[2,32,16,512]{3,2,1,0:T(8,128)} copy(f32[2,32,16,512]{3,2,1,0:T(8,128)} %bitcast.3) | data formatting | bytes 4194304

commit v7 on v6

--- a/solution.py
+++ b/solution.py
@@ -284,7 +284,7 @@
                 ww[rows, at : at + 128] = u
                 ww[below, at : at + 128] = v
                 wh[n, rows, 128 * k : 128 * k + 128] = w
-    for i in (2, 3, 5, 6, 7):
+    for i in (2, 3):
         snd_copy(i).wait_recv()
     e_copy.wait()
 
@@ -401,10 +401,13 @@
                     at = 64 * dg + 32 * part
                     flat[c, part, pl.ds(row, 32, stride=16), :] = rows[at : at + 32, 128 * c : 128 * c + 128]
 
+    def by_cross(i):
+        return jnp.logical_and(lax.rem(i, 2) == 0, i < 6)
+
     def relay(i):
         n, ii = lax.rem(i, 4), i // 4
 
-        @pl.when(lax.rem(i, 2) == 0)
+        @pl.when(by_cross(i))
         def _():
             at = dest_rows(n)
             for dg in range(2):
@@ -412,7 +415,7 @@
                 side[dg, ii, at, :] = side[dg, ii, at, :] + relay_in[i, dg]
                 row_copy(dg, i).start()
 
-        @pl.when(lax.rem(i, 2) == 1)
+        @pl.when(jnp.logical_not(by_cross(i)))
         def _():
             for dg in range(2):
                 opp_direct(dg, i).wait()
@@ -424,6 +427,8 @@
 
         @pl.when(i == 1)
         def _():
+            for late in range(5, 8):
+                snd_copy(late).wait_recv()
             a_copy(5).start()
             b_copy(5).start()
 
@@ -463,8 +468,17 @@
                             cross[dg, i] = value
                         else:
                             opp[i, dg] = value
-                            (opp_direct if nn % 2 else opp_cross)(dg, i).start()
-                if nn % 2 == 0:
+
+                            @pl.when(by_cross(i))
+                            def _():
+                                opp_cross(dg, i).start()
+
+                            @pl.when(jnp.logical_not(by_cross(i)))
+                            def _():
+                                opp_direct(dg, i).start()
+
+                @pl.when(by_cross(i))
+                def _():
                     for dg in range(2):
                         cross_copy(dg, i).start()
 
@@ -476,6 +490,11 @@
         def _():
             for dg in range(2):
                 row_copy(dg, 7).start()
+
+        @pl.when(i == 4)
+        def _():
+            for dg in range(2):
+                row_copy(dg, 6).start()
 
         @pl.when(i >= 4)
         def _():

time: 115 us -> 119 us (1.035)
  Pallas kernels: 111 us -> 116 us
    pallas_call x1, Pallas kernels: 111 us -> 116 us  [local(): pl.pallas_call(functools.partial(kernel, strips), in_specs=[hbm, hbm, hbm...]
where the time goes in v7:
time: 119 us
  Pallas kernels  116 us (97%)
  local copies, waits for them, and re-layouts  3.22 us (3%)
    pallas_call x1, Pallas kernels, local(): pl.pallas_call(functools.partial(kernel, strips), in_specs=[hbm, hbm, hbm...  116 us
    unnamed x1, local copies, waits for them, and re-layouts  3.22 us

profile of v7, /device:TPU:1, one launch (start us, length us, event | category | flops | bytes accessed | tf_op | source)
XLA Modules:
  0.0 118.8 jit_solution(8785236271755618731)
XLA Ops:
  0.0 115.6 %shard_map.73 = f32[2,512,512]{2,1,0:T(8,128)} custom-call(f32[2,512,1024]{2,1,0:T(8,128)} %bitcast.4, f32[32,2048]{1,0:T(8,128)} %phi_hbm.1, f32[2,2,256,256]{3,2,1,0:T(8,128)} %constant.4.clone.waves_hbm, f32[2,8,256]{2,1,0:T(8,128)} %constant.5.clone.tw_hbm, s32[1,32]{1,0:T(1,128)} %bitcast.5, f32[4,32]{1,0:T(4,128)} %tile_phase.1, s32[4]{0:T(128)} %tile_ids.1), custom_call_target="tpu_custom_call" | custom-call | flops 40000000000 | bytes 10485760 | tf_op jit(solution)/shard_map/pallas_call | solution.py:550
  115.6 3.2 %copy.9 = f32[2,32,16,512]{3,2,1,0:T(8,128)} copy(f32[2,32,16,512]{3,2,1,0:T(8,128)} %bitcast.3) | data formatting | bytes 4194304

commit v8 on v7

--- a/solution.py
+++ b/solution.py
@@ -374,10 +374,10 @@
                     near[dg, ii] = total[0:256]
                 else:
                     side[dg, ii] = total[0:256]
-                    row_copy(dg, 4 * ii + 1).start()
 
                     @pl.when(ii == 0)
                     def _():
+                        row_copy(dg, 1).start()
                         row_copy(dg, 3).start()
 
                 pp[2 * dg + dh, ii] = total[256:512]
@@ -402,7 +402,7 @@
                     flat[c, part, pl.ds(row, 32, stride=16), :] = rows[at : at + 32, 128 * c : 128 * c + 128]
 
     def by_cross(i):
-        return jnp.logical_and(lax.rem(i, 2) == 0, i < 6)
+        return jnp.logical_or(lax.rem(i, 2) == 0, i == 5)
 
     def relay(i):
         n, ii = lax.rem(i, 4), i // 4
@@ -486,15 +486,11 @@
         def _():
             relay(i - 1)
 
-        @pl.when(i == 3)
+        @pl.when(i == 2)
         def _():
             for dg in range(2):
                 row_copy(dg, 7).start()
 
-        @pl.when(i == 4)
-        def _():
-            for dg in range(2):
-                row_copy(dg, 6).start()
 
         @pl.when(i >= 4)
         def _():

time: 119 us -> 120 us (level)
  no operation moved by 1% of the time
where the time goes in v8:
time: 120 us
  Pallas kernels  117 us (98%)
  local copies, waits for them, and re-layouts  3.22 us (3%)
    pallas_call x1, Pallas kernels, local(): pl.pallas_call(functools.partial(kernel, strips), in_specs=[hbm, hbm, hbm...  117 us
    unnamed x1, local copies, waits for them, and re-layouts  3.22 us

profile of v8, /device:TPU:1, one launch (start us, length us, event | category | flops | bytes accessed | tf_op | source)
XLA Modules:
  0.0 119.8 jit_solution(10623430445416035840)
XLA Ops:
  0.0 116.5 %shard_map.73 = f32[2,512,512]{2,1,0:T(8,128)} custom-call(f32[2,512,1024]{2,1,0:T(8,128)} %bitcast.4, f32[32,2048]{1,0:T(8,128)} %phi_hbm.1, f32[2,2,256,256]{3,2,1,0:T(8,128)} %constant.4.clone.waves_hbm, f32[2,8,256]{2,1,0:T(8,128)} %constant.5.clone.tw_hbm, s32[1,32]{1,0:T(1,128)} %bitcast.5, f32[4,32]{1,0:T(4,128)} %tile_phase.1, s32[4]{0:T(128)} %tile_ids.1), custom_call_target="tpu_custom_call" | custom-call | flops 40000000000 | bytes 10485760 | tf_op jit(solution)/shard_map/pallas_call | solution.py:546
  116.5 3.2 %copy.9 = f32[2,32,16,512]{3,2,1,0:T(8,128)} copy(f32[2,32,16,512]{3,2,1,0:T(8,128)} %bitcast.3) | data formatting | bytes 4194304
